TPU v7x, 32 devices: a whole 2x2x4 slice. The times are simulated.
32 devices in a mesh: gx: 8 (over z, x), gy: 4 (over y, core).
Axes of the slice: x: 2, y: 2, z: 4, core: 2. Of those that a mesh axis runs over, the one named last changes fastest.
Arguments:
- amplitudes: float32 [2, 512, 128, 512], P(None, 'gx', None, 'gy'), may hold values from -6 to 6
- integrals: float32 [2, 32, 128, 128, 512], P(None, 'gy', None, 'gx'), may hold values from -0.046875 to 0.046875
- virt_count: int32 [8], replicated, may hold values from 24 to 128, as said below
- pair_irrep: int32 [8], replicated, may hold values from 0 to 7, as said below
- slab_index: int32 [1], replicated, may hold values from 0 to 15
- occ_energy: float32 [64], replicated, may hold values from -2 to -0.3
- virt_energy: float32 [512], replicated, may hold values from 0.1 to 3
Outputs:
- update: float32 [2, 512, 32, 128], P(None, 'gx', 'gy')
Inputs may be any that keep to these rules, and one draw needn't show every extreme that they name: `virt_count`: entry k counts the virtual orbitals of irrep k; they sum to 512 and the largest is exactly 128. `pair_irrep`: a permutation of the irreps.
All inputs are finite; a program needn't handle non-finite values.
Results may differ from a plain program's by a relative error of at most 0.0001.
Values sent between devices are 32-bit elements; how exact they have to be, the bound alone decides.
A program may use at most 192 MiB of HBM per device.

v0:
```python
import jax
import jax.numpy as jnp
from jax import lax
from jax.sharding import PartitionSpec as P

OCC = 64
VIRT = 512
SLAB = 32
IRREPS = 8
SYMS = 2
MAXIRR = 128


def irrep_of(positions, starts):
    return jnp.sum((positions[..., None] >= starts[1:]).astype(jnp.int32), axis=-1)


def lookup(entries, positions):
    picks = (positions[..., None] == jnp.arange(IRREPS, dtype=jnp.int32)).astype(entries.dtype)
    return jnp.sum(entries * picks, axis=-1)


def denominator_update(
    ladder, pair_rows, slab_rows, symmetry, slab_first, starts, virt_count, occ_energy, virt_energy
):
    per_irrep = OCC // IRREPS
    occ_irrep = pair_rows // (per_irrep * per_irrep)
    first_occ = per_irrep * occ_irrep + pair_rows % (per_irrep * per_irrep) // per_irrep
    second_occ = per_irrep * jnp.bitwise_xor(occ_irrep, symmetry) + pair_rows % per_irrep
    occ_sum = jnp.take(occ_energy, first_occ) + jnp.take(occ_energy, second_occ)
    slab_virt = SLAB * slab_first + slab_rows
    partner = jnp.bitwise_xor(irrep_of(slab_virt, starts), symmetry)
    block_start = lookup(starts, partner)
    block_count = lookup(virt_count, partner)
    slot_range = jnp.arange(MAXIRR, dtype=jnp.int32)
    partner_orbital = jnp.clip(block_start[:, None] + slot_range[None, :], 0, VIRT - 1)
    slot_valid = slot_range[None, :] < block_count[:, None]
    denominator = (
        occ_sum[:, None, None]
        - jnp.take(virt_energy, slab_virt)[None, :, None]
        - jnp.take(virt_energy, partner_orbital)[None]
    )
    return jnp.where(slot_valid[None], ladder / denominator, jnp.zeros_like(ladder))


def on_device(amplitudes, integrals, virt_count, pair_irrep, slab_index, occ_energy, virt_energy):
    starts = jnp.cumsum(virt_count) - virt_count
    handled = pair_irrep[:SYMS]
    pair_block = lax.axis_index("gx")
    virt_block = lax.axis_index("gy")
    slot_width = integrals.shape[3]
    slot_ids = pair_block * slot_width + jnp.arange(slot_width, dtype=jnp.int32)
    exchanged = lax.all_to_all(amplitudes, "gx", split_axis=2, concat_axis=1, tiled=True)
    piece = lax.all_gather(exchanged, "gy", axis=3, tiled=True)
    width = piece.shape[3]
    virt_ids = jnp.arange(width, dtype=jnp.int32)
    partner = jnp.bitwise_xor(irrep_of(virt_ids, starts)[None, :], handled[:, None])
    valid = slot_ids[None, :, None] < lookup(virt_count, partner)[:, None, :]
    masked = jnp.where(valid[:, None], piece, jnp.zeros_like(piece))
    ladder = lax.dot_general(
        masked,
        integrals,
        (((2, 3), (3, 4)), ((0,), (0,))),
        precision=lax.Precision.HIGHEST,
        preferred_element_type=jnp.float32,
    )
    by_slot = lax.psum_scatter(ladder, "gx", scatter_dimension=3, tiled=True)
    reduced = lax.all_to_all(by_slot, "gx", split_axis=1, concat_axis=3, tiled=True)
    pair_rows = pair_block * reduced.shape[1] + jnp.arange(reduced.shape[1], dtype=jnp.int32)
    slab_rows = virt_block * reduced.shape[2] + jnp.arange(reduced.shape[2], dtype=jnp.int32)
    updates = []
    for member in range(SYMS):
        updates.append(
            denominator_update(
                reduced[member],
                pair_rows,
                slab_rows,
                handled[member],
                slab_index[0],
                starts,
                virt_count,
                occ_energy,
                virt_energy,
            )
        )
    return jnp.stack(updates)


def solution(mesh):
    placed = (P(None, "gx", None, "gy"), P(None, "gy", None, "gx", None), P(), P(), P(), P(), P())
    return jax.shard_map(
        on_device, mesh=mesh, in_specs=placed, out_specs=P(None, "gx", "gy", None), check_vma=False
    )
```

profile of v0, /device:TPU:0, one launch (start us, length us, event | category | flops | bytes accessed | tf_op | source)
XLA Modules:
  0.0 673.1 jit_solution(428186920556085515)
XLA Ops:
  6.5 8.3 %copy.22 = f32[2,64,128,128]{3,1,0,2:T(8,128)S(1)} copy(f32[2,64,128,128]{3,2,1,0:T(8,128)} %param.13) | data formatting | bytes 16777216 | tf_op args[0]
  14.8 190.1 %all_to_all.33 = f32[2,64,128,128]{3,1,0,2:T(8,128)S(1)} all-to-all(f32[2,64,128,128]{3,1,0,2:T(8,128)S(1)} %copy.22), channel_id=1, replica_groups=mesh['gx'=8,'gy'=4] {'gx'}, dimensions={2} | all-to-all | bytes 16777216 | tf_op jit(solution)/shard_map/all_to_all | solution.py:53
  204.9 4.0 copy.23
  209.9 204.3 %all-gather.2.cloned.1.call-done = f32[2,512,16,512]{3,1,2,0:T(8,128)} async-done(((f32[2,512,16,128]{3,1,2,0:T(8,128)}), f32[2,512,16,512]{3,1,2,0:T(8,128)}) %all-gather.2.cloned.1.call-update) | async-done | bytes 33554448 | tf_op jit(solution)/shard_map/all_gather | solution.py:54
  414.2 121.9 %fusion.6 = f32[2,512,8,128]{1,3,2,0:T(8,128)} fusion(f32[2,8,128,16,512]{4,3,2,1,0:T(8,128)} %param.14, f32[2,512,16,512]{3,1,2,0:T(8,128)} %all-gather.2.cloned.1.call-done, pred[2,16,512]{2,1,0:T(8,128)(4,1)S(1)} %broadcast_compare_fusion), kind=kOutput, calls=%fused_computation.12 | convolution fusion | flops 103087603712 | bytes 104873984 | tf_op jit(solution)/shard_map/dot_general | solution.py:60
  536.8 0.6 gather_fusion.2
  537.5 0.6 fusion.24
  538.1 0.6 compare_select_fusion.4
  539.5 1.2 broadcast_xor_fusion.1
  541.2 83.5 %reduce-scatter.2.cloned.1.call-done = f32[2,512,8,16]{1,3,2,0:T(8,128)} async-done(((f32[2,512,8,128]{1,3,2,0:T(8,128)}), f32[2,512,8,16]{1,3,2,0:T(8,128)}) %reduce-scatter.2.cloned.1.call-update) | async-done | bytes 524304 | tf_op jit(solution)/shard_map/reduce_scatter | solution.py:67
  624.8 4.5 copy.25
  629.3 4.4 reshape.303
  633.6 4.4 all-to-all-start.1
  638.0 6.9 %gather_fusion.5 = f32[1024]{0:T(1024)S(1)} fusion(f32[512]{0:T(512)S(1)} %copy-done, s32[1024]{0:T(1024)S(1)} %bitcast_clamp_fusion), kind=kCustom, calls=%fused_computation.5.clone | custom fusion | bytes 12288 | tf_op jit(solution)/shard_map/jit(_take)/gather | solution.py:41
  644.9 0.8 gather_fusion.1
  645.7 0.8 gather_fusion
  646.5 0.8 gather_fusion.4
  647.2 6.9 %gather_fusion.3 = f32[1024]{0:T(1024)S(1)} fusion(f32[512]{0:T(512)S(1)} %copy-done, s32[1024]{0:T(1024)S(1)} %bitcast_clamp_fusion.1), kind=kCustom, calls=%fused_computation.2.clone | custom fusion | bytes 12288 | tf_op jit(solution)/shard_map/jit(_take)/gather | solution.py:41
  654.1 1.2 fusion.19
  656.0 1.9 reduce
  658.0 3.3 reshape.304
  661.3 2.8 copy.26
  664.2 0.8 fusion.11
  665.2 1.1 copy.27
  (41 shorter events, 3.1 us)
Async XLA Ops:
  6.5 530.3 %copy-start = (f32[512]{0:T(512)S(1)}, f32[512]{0:T(512)}, u32[]{:S(2)}) copy-start(f32[512]{0:T(512)} %param.19) | copy-start | bytes 6148
  6.5 202.7 %copy-start.3 = (s32[8]{0:T(128)S(1)}, s32[8]{0:T(128)}, u32[]{:S(2)}) copy-start(s32[8]{0:T(128)} %param.15) | copy-start | bytes 100
  6.5 203.1 %copy-start.2 = (s32[8]{0:T(128)S(1)}, s32[8]{0:T(128)}, u32[]{:S(2)}) copy-start(s32[8]{0:T(128)} %param.16) | copy-start | bytes 100
  6.5 407.7 %all-gather.2.cloned.1.call-start = ((), (), s32[]{:S(2)}) async-start(), calls=%async_computation.3 | async-start | bytes 41943040 | tf_op jit(solution)/shard_map/all_gather | solution.py:54
  209.0 415.8 %reduce-scatter.2.cloned.1.call-start = ((), (), s32[]{:S(2)}) async-start(), calls=%async_computation.4 | async-start | bytes 4718592 | tf_op jit(solution)/shard_map/reduce_scatter | solution.py:67
  209.9 435.0 %copy-start.1 = (f32[64]{0:T(128)S(1)}, f32[64]{0:T(128)}, u32[]{:S(2)}) copy-start(f32[64]{0:T(128)} %param.18) | copy-start | bytes 772
  633.6 21.9 %all-to-all-start.1 = ((f32[8,1,16384]{2,1,0:T(1,128)}), f32[8,1,16384]{2,1,0:T(1,128)S(1)}, u32[]{:S(2)}, u32[]{:S(2)}) async-start(f32[8,1,16384]{2,1,0:T(1,128)} %reshape.303), calls=%async_computation.2 | async-start | bytes 1048576 | tf_op jit(solution)/shard_map/all_to_all | solution.py:68
Sparse Core Ops, SparseCore 0:
  209.1 205.0 all-gather.1
  536.3 88.4 reduce-scatter.1
where the time goes:
time: 673 us
  waiting for transfers between devices  288 us (43%)
  blocking collectives  190 us (28%)
  matrix products  122 us (18%)
  local copies, waits for them, and re-layouts  46.4 us (7%)
  between operations  14.2 us (2%)
  other arithmetic  7.92 us (1%)
    all_gather x1, waiting for transfers between devices, on_device(): piece = lax.all_gather(exchanged, 'gy', axis=3, tiled=True)  204 us
    all_to_all x1, blocking collectives, on_device(): lax.all_to_all(amplitudes, 'gx', split_axis=2, concat_axis=1, tiled=True)  190 us
    dot_general x1, matrix products, on_device(): lax.dot_general(masked, integrals, (((2, 3), (3, 4)), ((0,), (0,))), prec...  122 us
    reduce_scatter x1, waiting for transfers between devices, on_device(): by_slot = lax.psum_scatter(ladder, 'gx', scatter_dimension=3, tiled=True)  83.5 us
    unnamed x11, local copies, waits for them, and re-layouts  16 us
    gather x2, local copies, waits for them, and re-layouts, denominator_update(): jnp.take(virt_energy, partner_orbital)[None]  13.7 us
  transfers between devices with their start and end apart: 3, of which 2 were waited for; matrix products, arithmetic and copies ran while one was open for 3% of the time, Pallas kernels for 0%

commit v1 on v0

v1 whole, which is shorter than its diff:
```python
import jax
import jax.numpy as jnp
from jax import lax
from jax.sharding import PartitionSpec as P

OCC = 64
VIRT = 512
SLAB = 32
IRREPS = 8
SYMS = 2
MAXIRR = 128
PARTS = 2


def irrep_of(positions, starts):
    return jnp.sum((positions[..., None] >= starts[1:]).astype(jnp.int32), axis=-1)


def lookup(entries, positions):
    picks = (positions[..., None] == jnp.arange(IRREPS, dtype=jnp.int32)).astype(entries.dtype)
    return jnp.sum(entries * picks, axis=-1)


def select_entries(entries, positions):
    picks = positions[..., None] == jnp.arange(entries.shape[0], dtype=jnp.int32)
    return jnp.sum(jnp.where(picks, entries, jnp.zeros_like(entries)), axis=-1)


def denominators(
    pair_rows, slab_rows, symmetry, slab_first, starts, virt_count, occ_energy, virt_energy
):
    per_irrep = OCC // IRREPS
    occ_irrep = pair_rows // (per_irrep * per_irrep)
    first_occ = per_irrep * occ_irrep + pair_rows % (per_irrep * per_irrep) // per_irrep
    second_occ = per_irrep * jnp.bitwise_xor(occ_irrep, symmetry) + pair_rows % per_irrep
    occ_sum = select_entries(occ_energy, first_occ) + select_entries(occ_energy, second_occ)
    slab_virt = SLAB * slab_first + slab_rows
    partner = jnp.bitwise_xor(irrep_of(slab_virt, starts), symmetry)
    block_start = lookup(starts, partner)
    block_count = lookup(virt_count, partner)
    slot_range = jnp.arange(MAXIRR, dtype=jnp.int32)
    partner_orbital = jnp.clip(block_start[:, None] + slot_range[None, :], 0, VIRT - 1)
    slot_valid = slot_range[None, :] < block_count[:, None]
    virt_first = select_entries(virt_energy, slab_virt)
    virt_second = select_entries(virt_energy, partner_orbital)
    return occ_sum, virt_first, virt_second, slot_valid


def on_device(amplitudes, integrals, virt_count, pair_irrep, slab_index, occ_energy, virt_energy):
    starts = jnp.cumsum(virt_count) - virt_count
    handled = pair_irrep[:SYMS]
    pair_block = lax.axis_index("gx")
    virt_block = lax.axis_index("gy")
    rows = amplitudes.shape[1]
    width = amplitudes.shape[3]
    slab = integrals.shape[1]
    slot_width = integrals.shape[3]
    part = rows // PARTS
    slot_ids = pair_block * slot_width + jnp.arange(slot_width, dtype=jnp.int32)
    virt_ids = virt_block * width + jnp.arange(width, dtype=jnp.int32)
    partner = jnp.bitwise_xor(irrep_of(virt_ids, starts)[None, :], handled[:, None])
    valid = slot_ids[None, :, None] < lookup(virt_count, partner)[:, None, :]
    pair_rows = pair_block * rows + jnp.arange(rows, dtype=jnp.int32)
    slab_rows = virt_block * slab + jnp.arange(slab, dtype=jnp.int32)
    energies = [
        denominators(
            pair_rows, slab_rows, handled[g], slab_index[0], starts, virt_count, occ_energy, virt_energy
        )
        for g in range(SYMS)
    ]
    updates, sent, masked = [], [], None
    for g in range(SYMS):
        for c in range(PARTS):
            mine = slice(c * part, (c + 1) * part)
            block = amplitudes[g, mine]
            if masked is not None:
                block, masked = lax.optimization_barrier((block, masked))
                sent.append(masked)
            exchanged = lax.all_to_all(block, "gx", split_axis=1, concat_axis=0, tiled=True)
            masked = jnp.where(valid[g][None], exchanged, jnp.zeros_like(exchanged))
    sent.append(masked)
    for g in range(SYMS):
        occ_sum, virt_first, virt_second, slot_valid = energies[g]
        for c in range(PARTS):
            mine = slice(c * part, (c + 1) * part)
            gathered = lax.all_gather(sent[g * PARTS + c], "gy", axis=2, tiled=True)
            ladder = lax.dot_general(
                gathered,
                integrals[g],
                (((1, 2), (2, 3)), ((), ())),
                precision=lax.Precision.HIGH,
                preferred_element_type=jnp.float32,
            )
            reduced = lax.psum_scatter(ladder, "gx", scatter_dimension=0, tiled=True)
            denominator = (
                occ_sum[mine, None, None] - virt_first[None, :, None] - virt_second[None]
            )
            updates.append(
                jnp.where(slot_valid[None], reduced / denominator, jnp.zeros_like(reduced))
            )
    return jnp.concatenate(updates).reshape(SYMS, rows, slab, MAXIRR)


def solution(mesh):
    placed = (P(None, "gx", None, "gy"), P(None, "gy", None, "gx", None), P(), P(), P(), P(), P())
    return jax.shard_map(
        on_device, mesh=mesh, in_specs=placed, out_specs=P(None, "gx", "gy", None), check_vma=False
    )
```

time: 673 us -> 599 us (0.89)
  blocking collectives: 190 us -> 103 us
  waiting for transfers between devices: 288 us -> 244 us
  local copies, waits for them, and re-layouts: 46.4 us -> 71 us
  matrix products: 122 us -> 134 us
  starting transfers between devices: 4.59 us -> 12.5 us
    all_gather x1 -> x4, waiting for transfers between devices: 204 us -> 0.06 us  [on_device(): gathered = lax.all_gather(sent[g * PARTS + c], 'gy', axis=2, tiled=True)]
    all_to_all x1 -> x2, blocking collectives: 190 us -> 103 us  [on_device(): lax.all_to_all(block, 'gx', split_axis=1, concat_axis=0, tiled=True)]
    all_to_all x1 -> x2, waiting for transfers between devices: 0.01 us -> 84.6 us  [on_device(): lax.all_to_all(block, 'gx', split_axis=1, concat_axis=0, tiled=True)]
    reduce_scatter x1 -> x4, waiting for transfers between devices: 83.5 us -> 159 us  [on_device(): reduced = lax.psum_scatter(ladder, 'gx', scatter_dimension=0, tiled=True)]
    slice x2 -> x5, local copies, waits for them, and re-layouts: 0.67 us -> 52.1 us  [the longest x1 45 us: on_device(): integrals[g]]
    gather x6 -> x0, local copies, waits for them, and re-layouts: 16.7 us -> none  [the longest x2 13.7 us: denominator_update(): jnp.take(virt_energy, partner_orbital)[None]]
    dot_general x1 -> x4, matrix products: 122 us -> 134 us  [on_device(): lax.dot_general(gathered, integrals[g], (((1, 2), (2, 3)), ((), ())), pre...]
    squeeze x0 -> x1, local copies, waits for them, and re-layouts: none -> 7.14 us  [on_device(): block = amplitudes[g, mine]]
  transfers between devices with their start and end apart: 3 -> 10, of which waited for: 2 -> 5; matrix products, arithmetic and copies ran while one was open for 3% -> 34% of each run, Pallas kernels for 0% -> 0%
where the time goes in v1:
time: 599 us; the launch traced here: 592 us
  waiting for transfers between devices  244 us (41%)
  matrix products  134 us (22%)
  blocking collectives  103 us (17%)
  local copies, waits for them, and re-layouts  71 us (12%)
  between operations  14.6 us (2%)
  other arithmetic  13.7 us (2%)
  starting transfers between devices  12.5 us (2%)
    reduce_scatter x4, waiting for transfers between devices, on_device(): reduced = lax.psum_scatter(ladder, 'gx', scatter_dimension=0, tiled=True)  159 us
    dot_general x4, matrix products, on_device(): lax.dot_general(gathered, integrals[g], (((1, 2), (2, 3)), ((), ())), pre...  134 us
    all_to_all x2, blocking collectives, on_device(): lax.all_to_all(block, 'gx', split_axis=1, concat_axis=0, tiled=True)  103 us
    all_to_all x2, waiting for transfers between devices, on_device(): lax.all_to_all(block, 'gx', split_axis=1, concat_axis=0, tiled=True)  84.6 us
    slice x1, local copies, waits for them, and re-layouts, on_device(): integrals[g]  45 us
  transfers between devices with their start and end apart: 10, of which 5 were waited for; matrix products, arithmetic and copies ran while one was open for 34% of the time, Pallas kernels for 0%

profile of v1, /device:TPU:0, one launch (start us, length us, event | category | flops | bytes accessed | tf_op | source)
XLA Modules:
  0.0 592.4 jit_solution(7827147042404103951)
XLA Ops:
  6.5 6.3 %fusion.23 = (f32[1,32,128,128]{3,2,1,0:T(8,128)S(1)}, f32[1,32,128,128]{3,2,1,0:T(8,128)}, f32[1,32,128,128]{3,2,1,0:T(8,128)}, f32[1,32,128,128]{3,2,1,0:T(8,128)}) fusion(f32[2,64,128,128]{3,2,1,0:T(8,128)} %param.7), kind=kLoop, calls=%fused_computation.84 | loop fusion | bytes 16777216 | tf_op jit(solution)/shard_map/slice | solution.py:75
  12.8 2.5 copy.65
  15.4 7.4 %all-to-all-start = ((f32[32,128,128]{2,0,1:T(8,128)}), f32[32,128,128]{2,0,1:T(8,128)S(1)}, u32[]{:S(2)}, u32[]{:S(2)}) async-start(f32[32,128,128]{2,0,1:T(8,128)} %bitcast.91), calls=%async_computation | async-start | bytes 4194304 | tf_op jit(solution)/shard_map/all_to_all | solution.py:79
  23.1 4.2 copy.66
  27.6 43.4 %all-to-all-done = f32[32,128,128]{2,0,1:T(8,128)S(1)} async-done(((f32[32,128,128]{2,0,1:T(8,128)}), f32[32,128,128]{2,0,1:T(8,128)S(1)}, u32[]{:S(2)}, u32[]{:S(2)}) %all-to-all-start) | async-done | bytes 2097184 | tf_op jit(solution)/shard_map/all_to_all | solution.py:79
  71.2 1.5 bitcast_select_fusion.3
  72.8 3.6 all-to-all-start.1
  76.4 7.1 %copy_bitcast_fusion.6 = (f32[32,128,128]{2,0,1:T(8,128)}, f32[32,128,128]{2,0,1:T(8,128)}) fusion(f32[1,32,128,128]{3,2,1,0:T(8,128)} %get-tuple-element.31, f32[1,32,128,128]{3,2,1,0:T(8,128)} %get-tuple-element.29), kind=kLoop, calls=%fused_computation.10 | loop fusion | bytes 8388608 | tf_op jit(solution)/shard_map/squeeze | solution.py:75
  83.6 41.2 %all-to-all-done.1 = f32[32,128,128]{2,0,1:T(8,128)S(1)} async-done(((f32[32,128,128]{2,0,1:T(8,128)}), f32[32,128,128]{2,0,1:T(8,128)S(1)}, u32[]{:S(2)}, u32[]{:S(2)}) %all-to-all-start.1) | async-done | bytes 2097184 | tf_op jit(solution)/shard_map/all_to_all | solution.py:79
  125.0 1.6 bitcast_select_fusion.2
  126.7 1.5 copy-done.1
  128.2 51.8 %all_to_all.72 = f32[32,128,128]{2,0,1:T(8,128)S(1)} all-to-all(f32[32,128,128]{2,0,1:T(8,128)S(1)} %copy-done.1), channel_id=1, replica_groups=mesh['gx'=8,'gy'=4] {'gx'}, dimensions={1} | all-to-all | bytes 4194304 | tf_op jit(solution)/shard_map/all_to_all | solution.py:79
  180.3 1.5 bitcast_select_fusion.1
  181.9 1.5 copy-done
  183.4 51.4 %all_to_all.73 = f32[32,128,128]{2,0,1:T(8,128)S(1)} all-to-all(f32[32,128,128]{2,0,1:T(8,128)S(1)} %copy-done), channel_id=1, replica_groups=mesh['gx'=8,'gy'=4] {'gx'}, dimensions={1} | all-to-all | bytes 4194304 | tf_op jit(solution)/shard_map/all_to_all | solution.py:79
  235.0 1.5 bitcast_select_fusion
  241.8 45.0 %fusion.22 = (f32[1,8,128,16,512]{4,3,2,1,0:T(8,128)}, f32[1,8,128,16,512]{4,3,2,1,0:T(8,128)}) fusion(f32[2,8,128,16,512]{4,3,2,1,0:T(8,128)} %param.8), kind=kLoop, calls=%fused_computation.83 | loop fusion | bytes 134217728 | tf_op jit(solution)/shard_map/slice | solution.py:89
  286.8 33.5 %fusion.14 = f32[256,8,128]{2,0,1:T(8,128)} fusion(f32[1,8,128,16,512]{4,3,2,1,0:T(8,128)} %get-tuple-element.26, f32[256,16,512]{2,0,1:T(8,128)} %all-gather.5.cloned.1.call-done), kind=kOutput, calls=%fused_computation.24 | convolution fusion | flops 12884901888 | bytes 42991616 | tf_op jit(solution)/shard_map/dot_general | solution.py:87
  320.5 33.4 %fusion.17 = f32[256,8,128]{2,0,1:T(8,128)} fusion(f32[1,8,128,16,512]{4,3,2,1,0:T(8,128)} %get-tuple-element.26, f32[256,16,512]{2,0,1:T(8,128)} %all-gather.7.cloned.1.call-done), kind=kOutput, calls=%fused_computation.25 | convolution fusion | flops 12884901888 | bytes 42991616 | tf_op jit(solution)/shard_map/dot_general | solution.py:87
  354.2 33.5 %fusion.8 = f32[256,8,128]{2,0,1:T(8,128)} fusion(f32[1,8,128,16,512]{4,3,2,1,0:T(8,128)} %get-tuple-element.27, f32[256,16,512]{2,0,1:T(8,128)} %all-gather.9.cloned.1.call-done), kind=kOutput, calls=%fused_computation.22 | convolution fusion | flops 12884901888 | bytes 42991616 | tf_op jit(solution)/shard_map/dot_general | solution.py:87
  388.0 33.4 %fusion.11 = f32[256,8,128]{2,0,1:T(8,128)} fusion(f32[1,8,128,16,512]{4,3,2,1,0:T(8,128)} %get-tuple-element.27, f32[256,16,512]{2,0,1:T(8,128)} %all-gather.11.cloned.1.call-done), kind=kOutput, calls=%fused_computation.23 | convolution fusion | flops 12884901888 | bytes 42991616 | tf_op jit(solution)/shard_map/dot_general | solution.py:87
  423.0 27.0 %reduce-scatter.7.cloned.1.call-done = f32[32,8,128]{2,0,1:T(8,128)} async-done(((f32[256,8,128]{2,0,1:T(8,128)}), f32[32,8,128]{2,0,1:T(8,128)}) %reduce-scatter.7.cloned.1.call-update) | async-done | bytes 131088 | tf_op jit(solution)/shard_map/reduce_scatter | solution.py:94
  451.1 65.3 %reduce-scatter.9.cloned.1.call-done = f32[32,8,128]{2,0,1:T(8,128)} async-done(((f32[256,8,128]{2,0,1:T(8,128)}), f32[32,8,128]{2,0,1:T(8,128)}) %reduce-scatter.9.cloned.1.call-update) | async-done | bytes 131088 | tf_op jit(solution)/shard_map/reduce_scatter | solution.py:94
  516.3 66.7 %reduce-scatter.11.cloned.1.call-done = f32[32,8,128]{2,0,1:T(8,128)} async-done(((f32[256,8,128]{2,0,1:T(8,128)}), f32[32,8,128]{2,0,1:T(8,128)}) %reduce-scatter.11.cloned.1.call-update) | async-done | bytes 131088 | tf_op jit(solution)/shard_map/reduce_scatter | solution.py:94
  (66 shorter events, 12.0 us)
Async XLA Ops:
  15.4 7.4 %copy-start.4 = (s32[8]{0:T(128)S(1)}, s32[8]{0:T(128)}, u32[]{:S(2)}) copy-start(s32[8]{0:T(128)} %param.9) | copy-start | bytes 100
  15.4 55.6 %all-to-all-start = ((f32[32,128,128]{2,0,1:T(8,128)}), f32[32,128,128]{2,0,1:T(8,128)S(1)}, u32[]{:S(2)}, u32[]{:S(2)}) async-start(f32[32,128,128]{2,0,1:T(8,128)} %bitcast.91), calls=%async_computation | async-start | bytes 4194304 | tf_op jit(solution)/shard_map/all_to_all | solution.py:79
  22.7 264.0 %all-gather.5.cloned.1.call-start = ((), (), s32[]{:S(2)}) async-start(), calls=%async_computation.8 | async-start | bytes 10485760 | tf_op jit(solution)/shard_map/all_gather | solution.py:86
  23.1 4.3 copy-start.3
  72.8 52.1 %all-to-all-start.1 = ((f32[32,128,128]{2,0,1:T(8,128)}), f32[32,128,128]{2,0,1:T(8,128)S(1)}, u32[]{:S(2)}, u32[]{:S(2)}) async-start(f32[32,128,128]{2,0,1:T(8,128)} %bitcast.88), calls=%async_computation.2 | async-start | bytes 4194304 | tf_op jit(solution)/shard_map/all_to_all | solution.py:79
  76.4 244.1 %all-gather.7.cloned.1.call-start = ((), (), s32[]{:S(2)}) async-start(), calls=%async_computation.10 | async-start | bytes 10485760 | tf_op jit(solution)/shard_map/all_gather | solution.py:86
  126.6 1.6 copy-start.1
  126.6 227.5 %all-gather.9.cloned.1.call-start = ((), (), s32[]{:S(2)}) async-start(), calls=%async_computation.12 | async-start | bytes 10485760 | tf_op jit(solution)/shard_map/all_gather | solution.py:86
  181.8 1.6 copy-start
  181.8 206.2 %all-gather.11.cloned.1.call-start = ((), (), s32[]{:S(2)}) async-start(), calls=%async_computation.14 | async-start | bytes 10485760 | tf_op jit(solution)/shard_map/all_gather | solution.py:86
  236.6 5.0 copy-start.5
  236.6 186.4 %reduce-scatter.5.cloned.1.call-start = ((), (), s32[]{:S(2)}) async-start(), calls=%async_computation.9 | async-start | bytes 1179648 | tf_op jit(solution)/shard_map/reduce_scatter | solution.py:94
  320.3 129.7 %reduce-scatter.7.cloned.1.call-start = ((), (), s32[]{:S(2)}) async-start(), calls=%async_computation.11 | async-start | bytes 1179648 | tf_op jit(solution)/shard_map/reduce_scatter | solution.py:94
  353.9 162.4 %reduce-scatter.9.cloned.1.call-start = ((), (), s32[]{:S(2)}) async-start(), calls=%async_computation.13 | async-start | bytes 1179648 | tf_op jit(solution)/shard_map/reduce_scatter | solution.py:94
  387.7 33.8 %copy-start.2 = (f32[512]{0:T(512)S(1)}, f32[512]{0:T(512)}, u32[]{:S(2)}) copy-start(f32[512]{0:T(512)} %param.13) | copy-start | bytes 6148
  387.7 195.4 %reduce-scatter.11.cloned.1.call-start = ((), (), s32[]{:S(2)}) async-start(), calls=%async_computation.15 | async-start | bytes 1179648 | tf_op jit(solution)/shard_map/reduce_scatter | solution.py:94
Sparse Core Ops, SparseCore 0:
  72.9 58.4 all-gather.4
  132.9 59.3 all-gather.6
  193.9 59.3 all-gather.8
  254.8 59.3 all-gather.10
  320.4 62.9 reduce-scatter.4
  387.0 62.9 reduce-scatter.6
  453.4 62.9 reduce-scatter.8
  520.1 62.8 reduce-scatter.10
